TPU v7x, 32 devices: a whole 2x2x4 slice. The times are simulated.
32 devices in a mesh: space: 8 (over z, x), kern: 4 (over y, core).
Axes of the slice: x: 2, y: 2, z: 4, core: 2. Of those that a mesh axis runs over, the one named last changes fastest.
Arguments:
- mask: bfloat16 [4096, 4096], P('space'), may hold values from -1 to 1
- kernels: float32 [2, 16, 512, 512], P(None, 'kern', 'space'), may hold values from -4 to 4
- target: int32 [1024, 1024], P('space'), may hold values 0 or 1
Outputs:
- gradient: float32 [4096, 4096], P('space')
- resist: float32 [1024, 1024], P('space')
All inputs are finite; a program needn't handle non-finite values. No bound on the sum of `target` on one device may be relied on, other than what follows from the above.
Results may differ from a plain program's by a relative error of at most 0.0003.
Values sent between devices are 32-bit elements; how exact they have to be, the bound alone decides.
A program may use at most 64 MiB of HBM per device.

v0:
```python
import jax
import jax.numpy as jnp
from jax import lax
from jax.sharding import PartitionSpec as P

N = 4096
B = 512
G = 1024
steepness = 8.0
threshold = 1.5
highest = lax.Precision.HIGHEST
block_limit = 1024


def phases(left, right, modulus):
    product = left[:, None] * right[None, :] % modulus
    return product.astype(jnp.float32) * (2.0 * jnp.pi / modulus)


def column_table(pixels, frequency, length):
    angle = phases(pixels, frequency, length)
    return jnp.concatenate([jnp.cos(angle), -jnp.sin(angle)], axis=1)


def row_table(pixels, frequency, length):
    angle = phases(pixels, frequency, length)
    return jnp.concatenate([jnp.cos(angle), -jnp.sin(angle)], axis=1) / length


def grid_table(frequency, points):
    angle = phases(frequency, jnp.arange(points, dtype=jnp.int32), points)
    return jnp.concatenate([jnp.cos(angle), jnp.sin(angle)], axis=1)


def forward_columns(mask, frequency):
    rows = mask.shape[0]
    span = min(block_limit, N)
    count = frequency.shape[0]

    def step(index, running):
        start = index * span
        table = column_table(start + jnp.arange(span, dtype=jnp.int32), frequency, N)
        piece = lax.dynamic_slice_in_dim(mask, start, span, 1).astype(jnp.float32)
        return running + lax.dot_general(table, piece, (((0,), (1,)), ((), ())), precision=highest)

    running = lax.fori_loop(0, N // span, step, jnp.zeros((2 * count, rows), jnp.float32))
    return running.reshape(2, count, rows)


def forward_rows(arrived):
    count = arrived.shape[1]
    flat = arrived.reshape(2 * count, N)
    frequency = jnp.arange(B, dtype=jnp.int32) - B // 2
    span = min(block_limit, N)

    def step(index, running):
        start = index * span
        table = row_table(start + jnp.arange(span, dtype=jnp.int32), frequency, N)
        piece = lax.dynamic_slice_in_dim(flat, start, span, 1)
        return running + jnp.dot(piece, table, precision=highest)

    running = lax.fori_loop(0, N // span, step, jnp.zeros((2 * count, 2 * B), jnp.float32))
    real_part = running[:count, :B] - running[count:, B:]
    imag_part = running[:count, B:] + running[count:, :B]
    return jnp.stack([real_part, imag_part])


def adjoint_rows(sum_re, sum_im):
    count = sum_re.shape[0]
    stacked = jnp.concatenate(
        [jnp.concatenate([sum_re, sum_im], axis=1), jnp.concatenate([sum_im, -sum_re], axis=1)],
        axis=0,
    )
    frequency = jnp.arange(B, dtype=jnp.int32) - B // 2
    span = min(block_limit, N)

    def step(index, output):
        start = index * span
        table = row_table(start + jnp.arange(span, dtype=jnp.int32), frequency, N)
        piece = lax.dot_general(stacked, table, (((1,), (1,)), ((), ())), precision=highest)
        return lax.dynamic_update_slice_in_dim(output, piece, start, 1)

    output = lax.fori_loop(0, N // span, step, jnp.zeros((2 * count, N), jnp.float32))
    return output.reshape(2, count, N)


def add_columns(total, spectrum, frequency):
    span = min(block_limit, N)

    def step(index, running):
        start = index * span
        table = column_table(start + jnp.arange(span, dtype=jnp.int32), frequency, N)
        piece = lax.dot_general(spectrum, table, (((0,), (1,)), ((), ())), precision=highest)
        current = lax.dynamic_slice_in_dim(running, start, span, 1)
        return lax.dynamic_update_slice_in_dim(running, current + piece, start, 1)

    return lax.fori_loop(0, N // span, step, total)


def local(mask, kernels, target):
    rows = mask.shape[0]
    kern_count = lax.axis_size("kern")
    space_count = lax.axis_size("space")
    group = lax.axis_index("kern")
    per_space = B // space_count
    per_group = per_space // kern_count
    frequency = jnp.arange(B, dtype=jnp.int32) - B // 2
    subset = (
        per_space * jnp.arange(space_count, dtype=jnp.int32)[:, None]
        + per_group * group
        + jnp.arange(per_group, dtype=jnp.int32)[None, :]
    )
    columns = forward_columns(mask, subset.reshape(-1) - B // 2)
    arrived = lax.all_to_all(columns, "space", split_axis=1, concat_axis=2, tiled=True)
    spectrum = lax.all_gather(forward_rows(arrived), "kern", axis=1, tiled=True)
    kern_swap = jnp.swapaxes(kernels, 1, 2)
    kernel_count = kern_swap.shape[2]
    spec_re = spectrum[0][:, None, :]
    spec_im = spectrum[1][:, None, :]
    prod_re = kern_swap[0] * spec_re - kern_swap[1] * spec_im
    prod_im = kern_swap[0] * spec_im + kern_swap[1] * spec_re
    grid = grid_table(frequency, G)
    lifted = jnp.dot(
        jnp.stack([prod_re, prod_im]).reshape(2 * per_space * kernel_count, B),
        grid,
        precision=highest,
    )
    lifted = lifted.reshape(2, per_space, kernel_count, 2 * G)
    coarse_re = lifted[0, :, :, :G] - lifted[1, :, :, G:]
    coarse_im = lifted[0, :, :, G:] + lifted[1, :, :, :G]
    coarse = jnp.stack([coarse_re, coarse_im], axis=1)
    gathered = lax.all_to_all(coarse, "space", split_axis=3, concat_axis=0, tiled=True)
    grid_rows = gathered.shape[3]
    image = lax.dot_general(
        gathered.reshape(B, 2 * kernel_count * grid_rows),
        grid,
        (((0,), (0,)), ((), ())),
        precision=highest,
    )
    image = image.reshape(2, kernel_count, grid_rows, 2 * G)
    field_re = image[0, :, :, :G] - image[1, :, :, G:]
    field_im = image[0, :, :, G:] + image[1, :, :, :G]
    partial_light = jnp.sum(field_re * field_re + field_im * field_im, axis=0) / (B * B)
    intensity = lax.psum(partial_light, "kern")
    resist = jax.nn.sigmoid(steepness * (intensity - threshold))
    slope = 2.0 * (resist - target.astype(jnp.float32)) * steepness * resist * (1.0 - resist)
    scale = 2.0 * slope / (B * B)
    grad_re = scale * field_re
    grad_im = scale * field_im
    mixed = jnp.stack(
        [
            jnp.concatenate([grad_re, grad_im], axis=-1),
            jnp.concatenate([grad_im, -grad_re], axis=-1),
        ]
    )
    mixed = mixed.reshape(2 * kernel_count * grid_rows, 2 * G)
    backward = lax.dot_general(grid, mixed, (((1,), (1,)), ((), ())), precision=highest)
    backward = backward.reshape(B, 2, kernel_count, grid_rows)
    returned = lax.all_to_all(backward, "space", split_axis=0, concat_axis=3, tiled=True)
    back_re = returned[:, 0]
    back_im = returned[:, 1]
    mixed_two = jnp.stack(
        [
            jnp.concatenate([back_re, back_im], axis=-1),
            jnp.concatenate([back_im, -back_re], axis=-1),
        ]
    )
    mixed_two = mixed_two.reshape(2 * per_space * kernel_count, 2 * G)
    spectral = lax.dot_general(mixed_two, grid, (((1,), (1,)), ((), ())), precision=highest)
    spectral = spectral.reshape(2, per_space, kernel_count, B)
    sum_re = jnp.sum(kern_swap[0] * spectral[0] + kern_swap[1] * spectral[1], axis=1)
    sum_im = jnp.sum(kern_swap[0] * spectral[1] - kern_swap[1] * spectral[0], axis=1)
    empty = jnp.zeros((rows, N), jnp.float32)
    shares = (
        lax.psum_scatter(sum_re, "kern", scatter_dimension=0, tiled=True),
        lax.psum_scatter(sum_im, "kern", scatter_dimension=0, tiled=True),
    )
    delta = adjoint_rows(shares[0], shares[1])
    landed = lax.all_to_all(delta, "space", split_axis=2, concat_axis=1, tiled=True)
    ordering = (
        per_group * jnp.arange(kern_count, dtype=jnp.int32)[:, None, None]
        + per_space * jnp.arange(space_count, dtype=jnp.int32)[None, :, None]
        + jnp.arange(per_group, dtype=jnp.int32)[None, None, :]
    )
    ordered_freq = ordering.reshape(-1) - B // 2
    piece = lax.all_gather(landed, "kern", axis=1, tiled=True)
    width = piece.shape[1]
    gradient = add_columns(empty, piece.reshape(2 * width, rows), ordered_freq)
    return (gradient, resist)


def solution(mesh):
    in_specs = (P("space", None), P(None, "kern", "space", None), P("space", None))
    out_specs = (P("space", None), P("space", None))
    return jax.shard_map(local, mesh=mesh, in_specs=in_specs, out_specs=out_specs, check_vma=False)
```

profile of v0, /device:TPU:0, one launch (start us, length us, event | category | flops | bytes accessed | tf_op | source)
XLA Modules:
  0.0 641.8 jit_solution(11022036640361063977)
XLA Ops:
  7.2 22.0 %while.66 = (s32[]{:T(128)}, f32[256,512]{1,0:T(8,128)S(1)}, bf16[512,4096]{1,0:T(8,128)(2,1)}, s32[8]{0:T(128)S(1)}, s32[]{:T(128)}, /*index=5*/s32[]{:T(128)}, s32[]{:T(128)}, s32[]{:T(128)}) while((s32[]{:T(128)}, f32[256,512]{1,0:T(8,128)S(1)}, bf16[512,4096]{1,0:T(8,128)(2,1)}, s32[8]{0:T(128)S(1)}, s32[]{:T(128)}, ...), condition=%wide.region_1.2_spmd.clone, body=%wide.region_0.1_spmd.clone.sunk | while | flops 1613104384 | bytes 4204733 | solution.py:46
  9.5 3.2 convolution_add_fusion.2
  15.0 3.2 convolution_add_fusion.2
  20.5 3.2 convolution_add_fusion.2
  30.4 7.3 %all-to-all-start = ((f32[2,128,512]{2,0,1:T(2,128)}), f32[2,128,512]{2,0,1:T(2,128)S(1)}, u32[]{:S(2)}, u32[]{:S(2)}) async-start(f32[2,128,512]{2,0,1:T(2,128)} %copy.57), calls=%async_computation | async-start | bytes 1048576 | tf_op jit(solution)/shard_map/all_to_all | solution.py:114
  37.7 9.6 %fusion.78 = (f32[512,1024]{1,0:T(8,128)S(1)}, f32[512,1024]{1,0:T(8,128)}) fusion(s32[512]{0:T(512)S(1)} %iota_add_fusion.6), kind=kLoop, calls=%fused_computation.130 | loop fusion | flops 7340032 | bytes 4196352 | tf_op jit(solution)/shard_map/cos | solution.py:32
  47.3 4.8 all-to-all-done
  53.6 47.6 %while.67 = (s32[]{:T(128)}, f32[32,1024]{1,0:T(8,128)S(1)}, f32[32,4096]{1,0:T(8,128)}, s32[]{:T(128)}, s32[]{:T(128)}, /*index=5*/s32[]{:T(128)}, s32[]{:T(128)}) while((s32[]{:T(128)}, f32[32,1024]{1,0:T(8,128)S(1)}, f32[32,4096]{1,0:T(8,128)}, s32[]{:T(128)}, s32[]{:T(128)}, /*index=5*/s32[]{:T(128)}, s32[]{:T(128)}) %tuple.199), condition=%wide.region_3.4_spmd.clone, body=%wide.region_2.3_spmd.clone.sunk | while | flops 412681728 | bytes 8794261 | solution.py:62
  53.9 8.3 %fusion.116 = (f32[1024,512]{1,0:T(8,128)S(1)}, f32[1024,512]{1,0:T(8,128)S(1)}) fusion(s32[512]{0:T(512)S(1)} %iota_add_fusion.17, s32[1024]{0:T(1024)S(1)} %iota_add_fusion.18), kind=kLoop, calls=%fused_computation.79.clone.1 | loop fusion | flops 7864320 | bytes 4200448 | tf_op jit(solution)/shard_map/while/body/eval_jaxpr/cos | solution.py:27
  62.2 3.5 fusion.117
  65.7 8.3 %fusion.116 = (f32[1024,512]{1,0:T(8,128)S(1)}, f32[1024,512]{1,0:T(8,128)S(1)}) fusion(s32[512]{0:T(512)S(1)} %iota_add_fusion.17, s32[1024]{0:T(1024)S(1)} %iota_add_fusion.18), kind=kLoop, calls=%fused_computation.79.clone.1 | loop fusion | flops 7864320 | bytes 4200448 | tf_op jit(solution)/shard_map/while/body/eval_jaxpr/cos | solution.py:27
  74.0 3.5 fusion.117
  77.6 8.3 %fusion.116 = (f32[1024,512]{1,0:T(8,128)S(1)}, f32[1024,512]{1,0:T(8,128)S(1)}) fusion(s32[512]{0:T(512)S(1)} %iota_add_fusion.17, s32[1024]{0:T(1024)S(1)} %iota_add_fusion.18), kind=kLoop, calls=%fused_computation.79.clone.1 | loop fusion | flops 7864320 | bytes 4200448 | tf_op jit(solution)/shard_map/while/body/eval_jaxpr/cos | solution.py:27
  85.9 3.5 fusion.117
  89.4 8.3 %fusion.116 = (f32[1024,512]{1,0:T(8,128)S(1)}, f32[1024,512]{1,0:T(8,128)S(1)}) fusion(s32[512]{0:T(512)S(1)} %iota_add_fusion.17, s32[1024]{0:T(1024)S(1)} %iota_add_fusion.18), kind=kLoop, calls=%fused_computation.79.clone.1 | loop fusion | flops 7864320 | bytes 4200448 | tf_op jit(solution)/shard_map/while/body/eval_jaxpr/cos | solution.py:27
  97.7 3.5 fusion.117
  101.3 6.2 all_gather.6
  107.7 6.9 %fusion.61 = f32[2,64,4,2048]{3,1,2,0:T(8,128)S(1)} fusion(f32[512,1024]{1,0:T(8,128)S(1)} %copy-done.2, f32[512,1024]{1,0:T(8,128)S(1)} %get-tuple-element.572, f32[1,64,4,512]{3,1,2,0:T(8,128)S(1)} %get-tuple-element.563, f32[1,64,4,512]{3,1,2,0:T(8,128)S(1)} %get-tuple-element.562), kind=kOutput, calls=%fused_computation.97 | convolution fusion | flops 6443761664 | bytes 9437184 | tf_op jit(solution)/shard_map/dot_general | solution.py:123
  116.4 4.8 copy.60
  121.2 7.8 %reshape.172 = f32[8,1,65536]{2,1,0:T(1,128)} reshape(f32[1024,2,4,64]{3,2,1,0:T(4,128)} %bitcast.117) | data formatting | bytes 4194304
  129.0 53.8 %all_to_all.66 = f32[8,1,65536]{2,1,0:T(1,128)} all-to-all(f32[8,1,65536]{2,1,0:T(1,128)} %reshape.172), channel_id=1, replica_groups=mesh['space'=8,'kern'=4] {'space'}, dimensions={0} | all-to-all | bytes 4194304 | tf_op jit(solution)/shard_map/all_to_all | solution.py:132
  183.3 8.5 %reduce = f32[8,65536]{1,0:T(8,128)} reduce(f32[8,1,65536]{2,1,0:T(1,128)} %all_to_all.66, f32[]{:T(128)} %broadcast.375), dimensions={1}, to_apply=%all_to_all.51.reduce_sub_computation | reduce | bytes 4194308 | tf_op jit(solution)/shard_map/all_to_all | solution.py:132
  191.9 6.5 %reshape.173 = f32[1024,2,4,64]{3,2,1,0:T(4,128)} reshape(f32[8,65536]{1,0:T(8,128)} %reduce) | data formatting | bytes 4194304
  198.3 4.8 copy.61
  209.2 16.7 %fusion.59 = f32[2,4,128,2048]{3,2,1,0:T(8,128)S(1)} fusion(f32[2,4,128,512]{3,2,1,0:T(8,128)} %bitcast.122, f32[512,1024]{1,0:T(8,128)} %get-tuple-element.573, f32[512,1024]{1,0:T(8,128)S(1)} %get-tuple-element.572), kind=kOutput, calls=%fused_computation.95 | convolution fusion | flops 12885950464 | bytes 14680064 | tf_op jit(solution)/shard_map/dot_general | solution.py:134
  230.2 32.4 %all-reduce.2.cloned.1.call-done = f32[128,1024]{1,0:T(8,128)} async-done(((f32[128,1024]{1,0:T(8,128)}), f32[128,1024]{1,0:T(8,128)}) %all-reduce.2.cloned.1.call-update) | async-done | bytes 524304 | tf_op jit(solution)/shard_map/psum | solution.py:144
  264.8 4.5 fusion.88
  269.4 3.9 maximum_bitcast_fusion
  273.3 15.5 %fusion.54 = f32[512,2,4,128]{3,0,2,1:T(8,128)S(1)} fusion(f32[1,4,128,2048]{3,2,1,0:T(8,128)} %get-tuple-element.561, f32[1,4,128,2048]{3,2,1,0:T(8,128)} %get-tuple-element.560, f32[512,1024]{1,0:T(8,128)S(1)} %copy-done.3, f32[512,1024]{1,0:T(8,128)S(1)} %get-tuple-element.572), kind=kOutput, calls=%fused_computation.86 | convolution fusion | flops 12888047616 | bytes 14680064 | tf_op jit(solution)/shard_map/dot_general | solution.py:157
  290.1 53.1 %all_to_all.67 = f32[512,2,4,128]{3,2,1,0:T(4,128)S(1)} all-to-all(f32[512,2,4,128]{3,2,1,0:T(4,128)S(1)} %copy.63), channel_id=1, replica_groups=mesh['space'=8,'kern'=4] {'space'}, dimensions={0} | all-to-all | bytes 4194304 | tf_op jit(solution)/shard_map/all_to_all | solution.py:159
  351.5 4.7 copy.65
  356.2 5.3 reshape.168
  361.6 8.9 %fusion.71 = f32[512,512]{1,0:T(8,128)S(1)} fusion(f32[512,2048]{1,0:T(8,128)} %reshape.168, f32[512,1024]{1,0:T(8,128)} %get-tuple-element.573, f32[512,1024]{1,0:T(8,128)S(1)} %get-tuple-element.572), kind=kOutput, calls=%fused_computation.117 | convolution fusion | flops 6443499520 | bytes 9437184 | tf_op jit(solution)/shard_map/dot_general | solution.py:169
  372.8 17.0 %reduce-scatter.3.cloned.1.call-done = f32[16,512]{1,0:T(8,128)} async-done(((f32[64,512]{1,0:T(8,128)}), f32[16,512]{1,0:T(8,128)}) %reduce-scatter.3.cloned.1.call-update) | async-done | bytes 32784 | tf_op jit(solution)/shard_map/reduce_scatter | solution.py:175
  390.5 21.9 %reduce-scatter.5.cloned.1.call-done = f32[16,512]{1,0:T(8,128)} async-done(((f32[64,512]{1,0:T(8,128)}), f32[16,512]{1,0:T(8,128)}) %reduce-scatter.5.cloned.1.call-update) | async-done | bytes 32784 | tf_op jit(solution)/shard_map/reduce_scatter | solution.py:176
  413.3 49.2 %while.64 = (s32[]{:T(128)}, f32[32,4096]{1,0:T(8,128)S(1)}, f32[32,1024]{1,0:T(8,128)S(1)}, s32[]{:T(128)}, s32[]{:T(128)}, /*index=5*/s32[]{:T(128)}, s32[]{:T(128)}) while((s32[]{:T(128)}, f32[32,4096]{1,0:T(8,128)S(1)}, f32[32,1024]{1,0:T(8,128)S(1)}, s32[]{:T(128)}, s32[]{:T(128)}, /*index=5*/s32[]{:T(128)}, ...), condition=%wide.region_11.12_spmd.clone, body=%wide.region_10.11_spmd.clone.sunk | while | flops 412616192 | bytes 8663171 | solution.py:83
  413.5 8.3 %fusion.107 = (f32[1024,512]{1,0:T(8,128)S(1)}, f32[1024,512]{1,0:T(8,128)S(1)}) fusion(s32[512]{0:T(512)S(1)} %iota_add_fusion.13, s32[1024]{0:T(1024)S(1)} %iota_add_fusion.14), kind=kLoop, calls=%fused_computation.20.clone.1 | loop fusion | flops 7864320 | bytes 4200448 | tf_op jit(solution)/shard_map/while/body/eval_jaxpr/cos | solution.py:27
  421.8 3.9 fusion.108
  425.8 8.3 %fusion.107 = (f32[1024,512]{1,0:T(8,128)S(1)}, f32[1024,512]{1,0:T(8,128)S(1)}) fusion(s32[512]{0:T(512)S(1)} %iota_add_fusion.13, s32[1024]{0:T(1024)S(1)} %iota_add_fusion.14), kind=kLoop, calls=%fused_computation.20.clone.1 | loop fusion | flops 7864320 | bytes 4200448 | tf_op jit(solution)/shard_map/while/body/eval_jaxpr/cos | solution.py:27
  434.1 3.9 fusion.108
  438.0 8.3 %fusion.107 = (f32[1024,512]{1,0:T(8,128)S(1)}, f32[1024,512]{1,0:T(8,128)S(1)}) fusion(s32[512]{0:T(512)S(1)} %iota_add_fusion.13, s32[1024]{0:T(1024)S(1)} %iota_add_fusion.14), kind=kLoop, calls=%fused_computation.20.clone.1 | loop fusion | flops 7864320 | bytes 4200448 | tf_op jit(solution)/shard_map/while/body/eval_jaxpr/cos | solution.py:27
  446.3 3.9 fusion.108
  450.3 8.3 %fusion.107 = (f32[1024,512]{1,0:T(8,128)S(1)}, f32[1024,512]{1,0:T(8,128)S(1)}) fusion(s32[512]{0:T(512)S(1)} %iota_add_fusion.13, s32[1024]{0:T(1024)S(1)} %iota_add_fusion.14), kind=kLoop, calls=%fused_computation.20.clone.1 | loop fusion | flops 7864320 | bytes 4200448 | tf_op jit(solution)/shard_map/while/body/eval_jaxpr/cos | solution.py:27
  458.6 3.9 fusion.108
  462.5 4.3 copy.70
  466.8 7.4 %reshape.174 = f32[8,1,16384]{2,1,0:T(1,128)S(1)} reshape(f32[4096,2,16]{2,1,0:T(2,128)} %bitcast.119) | data formatting | bytes 1048576
  474.2 19.3 %all_to_all.68 = f32[8,1,16384]{2,1,0:T(1,128)S(1)} all-to-all(f32[8,1,16384]{2,1,0:T(1,128)S(1)} %reshape.174), channel_id=1, replica_groups=mesh['space'=8,'kern'=4] {'space'}, dimensions={0} | all-to-all | bytes 1048576 | tf_op jit(solution)/shard_map/all_to_all | solution.py:179
  495.4 7.6 %reshape.175 = f32[4096,2,16]{2,1,0:T(2,128)} reshape(f32[8,16384]{1,0:T(8,128)S(1)} %reduce.1) | data formatting | bytes 1048576
  503.0 6.3 copy.76
  509.4 20.8 %all-gather.2.cloned.1.call-done = f32[2,512,512]{2,1,0:T(8,128)} async-done(((f32[2,128,512]{2,1,0:T(8,128)}), f32[2,512,512]{2,1,0:T(8,128)}) %all-gather.2.cloned.1.call-update) | async-done | bytes 2097168 | tf_op jit(solution)/shard_map/all_gather | solution.py:186
  530.2 4.4 broadcast_in_dim.45.clone
  534.6 100.2 %while.65 = (s32[]{:T(128)}, f32[512,4096]{1,0:T(8,128)}, f32[1024,512]{1,0:T(8,128)}, s32[4,8]{1,0:T(4,128)S(1)}, s32[]{:T(128)}, /*index=5*/s32[]{:T(128)}, s32[]{:T(128)}, s32[]{:T(128)}) while((s32[]{:T(128)}, f32[512,4096]{1,0:T(8,128)}, f32[1024,512]{1,0:T(8,128)}, s32[4,8]{1,0:T(4,128)S(1)}, s32[]{:T(128)}, ...), condition=%wide.region_13.14_spmd.clone, body=%wide.region_12.13_spmd.clone.sunk | while | flops 6451890176 | bytes 39862572 | solution.py:97
  535.0 3.2 constant_dynamic-slice_fusion.2
  540.2 8.3 %fusion.111 = (f32[1024,512]{1,0:T(8,128)S(1)}, f32[1024,512]{1,0:T(8,128)S(1)}) fusion(s32[512]{0:T(512)S(1)} %sub.133, s32[1024]{0:T(1024)S(1)} %iota_add_fusion.15), kind=kLoop, calls=%fused_computation.39.clone.1 | loop fusion | flops 7864320 | bytes 4200448 | tf_op jit(solution)/shard_map/while/body/eval_jaxpr/cos | solution.py:22
  548.5 8.0 %bitcast_add_fusion.2 = f32[512,1024]{0,1:T(8,128)} fusion(f32[512,1024]{0,1:T(8,128)S(1)} %copy.92, f32[1024,512]{1,0:T(8,128)S(1)} %copy-done.1, f32[1024,512]{1,0:T(8,128)S(1)} %get-tuple-element.665, f32[1024,512]{1,0:T(8,128)S(1)} %get-tuple-element.666), kind=kOutput, calls=%fused_computation.37.clone.1 | convolution fusion | flops 6444023808 | bytes 10485760 | tf_op jit(solution)/shard_map/while/body/eval_jaxpr/dot_general | solution.py:93
  560.0 3.2 constant_dynamic-slice_fusion.2
  565.1 8.3 %fusion.111 = (f32[1024,512]{1,0:T(8,128)S(1)}, f32[1024,512]{1,0:T(8,128)S(1)}) fusion(s32[512]{0:T(512)S(1)} %sub.133, s32[1024]{0:T(1024)S(1)} %iota_add_fusion.15), kind=kLoop, calls=%fused_computation.39.clone.1 | loop fusion | flops 7864320 | bytes 4200448 | tf_op jit(solution)/shard_map/while/body/eval_jaxpr/cos | solution.py:22
  573.4 8.0 %bitcast_add_fusion.2 = f32[512,1024]{0,1:T(8,128)} fusion(f32[512,1024]{0,1:T(8,128)S(1)} %copy.92, f32[1024,512]{1,0:T(8,128)S(1)} %copy-done.1, f32[1024,512]{1,0:T(8,128)S(1)} %get-tuple-element.665, f32[1024,512]{1,0:T(8,128)S(1)} %get-tuple-element.666), kind=kOutput, calls=%fused_computation.37.clone.1 | convolution fusion | flops 6444023808 | bytes 10485760 | tf_op jit(solution)/shard_map/while/body/eval_jaxpr/dot_general | solution.py:93
  585.0 3.2 constant_dynamic-slice_fusion.2
  590.1 8.3 %fusion.111 = (f32[1024,512]{1,0:T(8,128)S(1)}, f32[1024,512]{1,0:T(8,128)S(1)}) fusion(s32[512]{0:T(512)S(1)} %sub.133, s32[1024]{0:T(1024)S(1)} %iota_add_fusion.15), kind=kLoop, calls=%fused_computation.39.clone.1 | loop fusion | flops 7864320 | bytes 4200448 | tf_op jit(solution)/shard_map/while/body/eval_jaxpr/cos | solution.py:22
  598.4 8.0 %bitcast_add_fusion.2 = f32[512,1024]{0,1:T(8,128)} fusion(f32[512,1024]{0,1:T(8,128)S(1)} %copy.92, f32[1024,512]{1,0:T(8,128)S(1)} %copy-done.1, f32[1024,512]{1,0:T(8,128)S(1)} %get-tuple-element.665, f32[1024,512]{1,0:T(8,128)S(1)} %get-tuple-element.666), kind=kOutput, calls=%fused_computation.37.clone.1 | convolution fusion | flops 6444023808 | bytes 10485760 | tf_op jit(solution)/shard_map/while/body/eval_jaxpr/dot_general | solution.py:93
  610.0 3.2 constant_dynamic-slice_fusion.2
  615.1 8.3 %fusion.111 = (f32[1024,512]{1,0:T(8,128)S(1)}, f32[1024,512]{1,0:T(8,128)S(1)}) fusion(s32[512]{0:T(512)S(1)} %sub.133, s32[1024]{0:T(1024)S(1)} %iota_add_fusion.15), kind=kLoop, calls=%fused_computation.39.clone.1 | loop fusion | flops 7864320 | bytes 4200448 | tf_op jit(solution)/shard_map/while/body/eval_jaxpr/cos | solution.py:22
  623.4 8.0 %bitcast_add_fusion.2 = f32[512,1024]{0,1:T(8,128)} fusion(f32[512,1024]{0,1:T(8,128)S(1)} %copy.92, f32[1024,512]{1,0:T(8,128)S(1)} %copy-done.1, f32[1024,512]{1,0:T(8,128)S(1)} %get-tuple-element.665, f32[1024,512]{1,0:T(8,128)S(1)} %get-tuple-element.666), kind=kOutput, calls=%fused_computation.37.clone.1 | convolution fusion | flops 6444023808 | bytes 10485760 | tf_op jit(solution)/shard_map/while/body/eval_jaxpr/dot_general | solution.py:93
  (121 shorter events, 67.7 us)
Async XLA Ops:
  30.4 21.7 %all-to-all-start = ((f32[2,128,512]{2,0,1:T(2,128)}), f32[2,128,512]{2,0,1:T(2,128)S(1)}, u32[]{:S(2)}, u32[]{:S(2)}) async-start(f32[2,128,512]{2,0,1:T(2,128)} %copy.57), calls=%async_computation | async-start | bytes 1048576 | tf_op jit(solution)/shard_map/all_to_all | solution.py:114
  37.6 225.0 %all-reduce.2.cloned.1.call-start = ((), (), s32[]{:S(2)}) async-start(), calls=%async_computation.6 | async-start | bytes 1048576 | tf_op jit(solution)/shard_map/psum | solution.py:144
  53.6 53.8 %copy-start.5 = (f32[2,4,64,512]{3,2,1,0:T(8,128)S(1)}, f32[2,4,64,512]{3,2,1,0:T(8,128)}, u32[]{:S(2)}) copy-start(f32[2,4,64,512]{3,2,1,0:T(8,128)} %param.12) | copy-start | bytes 3145732
  101.2 6.5 %copy-start.2 = (f32[512,1024]{1,0:T(8,128)S(1)}, f32[512,1024]{1,0:T(8,128)}, u32[]{:S(2)}) copy-start(f32[512,1024]{1,0:T(8,128)} %get-tuple-element.573) | copy-start | bytes 6291460
  225.9 3.4 copy-start
  230.2 159.6 %reduce-scatter.3.cloned.1.call-start = ((), (), s32[]{:S(2)}) async-start(), calls=%async_computation.7 | async-start | bytes 163840 | tf_op jit(solution)/shard_map/reduce_scatter | solution.py:175
  269.3 4.0 copy-start.3
  348.5 1.9 copy-start.4
  372.0 40.5 %reduce-scatter.5.cloned.1.call-start = ((), (), s32[]{:S(2)}) async-start(), calls=%async_computation.8 | async-start | bytes 163840 | tf_op jit(solution)/shard_map/reduce_scatter | solution.py:176
  372.7 157.5 %all-gather.2.cloned.1.call-start = ((), (), s32[]{:S(2)}) async-start(), calls=%async_computation.9 | async-start | bytes 2621440 | tf_op jit(solution)/shard_map/all_gather | solution.py:186
  540.1 8.3 %copy-start.1 = (f32[1024,512]{1,0:T(8,128)S(1)}, f32[1024,512]{1,0:T(8,128)}, u32[]{:S(2)}) copy-start(f32[1024,512]{1,0:T(8,128)} %get-tuple-element.762) | copy-start | bytes 6291460 | tf_op jit(solution)/shard_map/while
  565.1 8.3 %copy-start.1 = (f32[1024,512]{1,0:T(8,128)S(1)}, f32[1024,512]{1,0:T(8,128)}, u32[]{:S(2)}) copy-start(f32[1024,512]{1,0:T(8,128)} %get-tuple-element.762) | copy-start | bytes 6291460 | tf_op jit(solution)/shard_map/while
  590.1 8.3 %copy-start.1 = (f32[1024,512]{1,0:T(8,128)S(1)}, f32[1024,512]{1,0:T(8,128)}, u32[]{:S(2)}) copy-start(f32[1024,512]{1,0:T(8,128)} %get-tuple-element.762) | copy-start | bytes 6291460 | tf_op jit(solution)/shard_map/while
  615.1 8.3 %copy-start.1 = (f32[1024,512]{1,0:T(8,128)S(1)}, f32[1024,512]{1,0:T(8,128)}, u32[]{:S(2)}) copy-start(f32[1024,512]{1,0:T(8,128)} %get-tuple-element.762) | copy-start | bytes 6291460 | tf_op jit(solution)/shard_map/while
Sparse Core Ops, SparseCore 0:
  230.3 32.2 all-reduce.1
  372.1 17.5 reduce-scatter.2
  392.9 19.5 reduce-scatter.4
  509.4 20.7 all-gather.1
where the time goes:
time: 649 us; the launch traced here: 642 us
  other arithmetic  149 us (23%)
  blocking collectives  132 us (20%)
  matrix products  122 us (19%)
  local copies, waits for them, and re-layouts  118 us (18%)
  waiting for transfers between devices  97.6 us (15%)
  between operations  14.5 us (2%)
  starting transfers between devices  7.41 us (1%)
    cos x8, other arithmetic, row_table(): return jnp.concatenate([jnp.cos(angle), -jnp.sin(angle)], axis=1) / length  66.3 us
    all_to_all x1, blocking collectives, local(): lax.all_to_all(coarse, 'space', split_axis=3, concat_axis=0, tiled=True)  53.8 us
    all_to_all x1, blocking collectives, local(): lax.all_to_all(backward, 'space', split_axis=0, concat_axis=3, tiled=True)  53.1 us
    cos x8, other arithmetic, column_table(): return jnp.concatenate([jnp.cos(angle), -jnp.sin(angle)], axis=1)  41.7 us
    unnamed x15, local copies, waits for them, and re-layouts  33.1 us
    psum x1, waiting for transfers between devices, local(): intensity = lax.psum(partial_light, 'kern')  32.4 us
    dot_general x4, matrix products, step(): lax.dot_general(spectrum, table, (((0,), (1,)), ((), ())), precision=high...  32.1 us
    reduce_scatter x1, waiting for transfers between devices, local(): lax.psum_scatter(sum_im, 'kern', scatter_dimension=0, tiled=True)  21.9 us
  transfers between devices with their start and end apart: 5, of which 5 were waited for; matrix products, arithmetic and copies ran while one was open for 2% of the time, Pallas kernels for 0%

commit v1 on v0

--- a/solution.py
+++ b/solution.py
@@ -141,7 +141,11 @@
     field_re = image[0, :, :, :G] - image[1, :, :, G:]
     field_im = image[0, :, :, G:] + image[1, :, :, :G]
     partial_light = jnp.sum(field_re * field_re + field_im * field_im, axis=0) / (B * B)
-    intensity = lax.psum(partial_light, "kern")
+    intensity = partial_light
+    for hop in (1, 2):
+        intensity = intensity + lax.ppermute(
+            intensity, "kern", [(dev, dev ^ hop) for dev in range(4)]
+        )
     resist = jax.nn.sigmoid(steepness * (intensity - threshold))
     slope = 2.0 * (resist - target.astype(jnp.float32)) * steepness * resist * (1.0 - resist)
     scale = 2.0 * slope / (B * B)

time: 649 us -> 624 us (0.961)
  waiting for transfers between devices: 97.6 us -> 80.5 us
    psum x1 -> x0, waiting for transfers between devices: 32.4 us -> none  [local(): intensity = lax.psum(partial_light, 'kern')]
    ppermute x0 -> x2, waiting for transfers between devices: none -> 14.3 us  [local(): lax.ppermute(intensity, 'kern', [(dev, dev ^ hop) for dev in range(4)])]
  transfers between devices with their start and end apart: 5 -> 6, of which waited for: 5 -> 6; matrix products, arithmetic and copies ran while one was open for 2% -> 2% of each run, Pallas kernels for 0% -> 0%
where the time goes in v1:
time: 624 us; the launch traced here: 617 us
  other arithmetic  144 us (23%)
  blocking collectives  131 us (21%)
  matrix products  121 us (19%)
  local copies, waits for them, and re-layouts  115 us (18%)
  waiting for transfers between devices  80.5 us (13%)
  between operations  14.5 us (2%)
  starting transfers between devices  9.02 us (1%)
    cos x8, other arithmetic, row_table(): return jnp.concatenate([jnp.cos(angle), -jnp.sin(angle)], axis=1) / length  66.3 us
    all_to_all x1, blocking collectives, local(): lax.all_to_all(coarse, 'space', split_axis=3, concat_axis=0, tiled=True)  53.8 us
    all_to_all x1, blocking collectives, local(): lax.all_to_all(backward, 'space', split_axis=0, concat_axis=3, tiled=True)  51.6 us
    cos x8, other arithmetic, column_table(): return jnp.concatenate([jnp.cos(angle), -jnp.sin(angle)], axis=1)  41.7 us
    dot_general x4, matrix products, step(): lax.dot_general(spectrum, table, (((0,), (1,)), ((), ())), precision=high...  32 us
    unnamed x15, local copies, waits for them, and re-layouts  30.9 us
    reduce_scatter x1, waiting for transfers between devices, local(): lax.psum_scatter(sum_im, 'kern', scatter_dimension=0, tiled=True)  22 us
    all_gather x1, waiting for transfers between devices, local(): piece = lax.all_gather(landed, 'kern', axis=1, tiled=True)  20.8 us
  transfers between devices with their start and end apart: 6, of which 6 were waited for; matrix products, arithmetic and copies ran while one was open for 2% of the time, Pallas kernels for 0%

profile of v1, /device:TPU:0, one launch (start us, length us, event | category | flops | bytes accessed | tf_op | source)
XLA Modules:
  0.0 616.9 jit_solution(5234536926072791631)
XLA Ops:
  7.2 22.0 %while.66 = (s32[]{:T(128)}, f32[256,512]{1,0:T(8,128)S(1)}, bf16[512,4096]{1,0:T(8,128)(2,1)}, s32[8]{0:T(128)S(1)}, s32[]{:T(128)}, /*index=5*/s32[]{:T(128)}, s32[]{:T(128)}, s32[]{:T(128)}) while((s32[]{:T(128)}, f32[256,512]{1,0:T(8,128)S(1)}, bf16[512,4096]{1,0:T(8,128)(2,1)}, s32[8]{0:T(128)S(1)}, s32[]{:T(128)}, ...), condition=%wide.region_1.2_spmd.clone, body=%wide.region_0.1_spmd.clone.sunk | while | flops 1613104384 | bytes 4204733 | solution.py:46
  9.5 3.2 convolution_add_fusion.2
  15.0 3.2 convolution_add_fusion.2
  20.5 3.2 convolution_add_fusion.2
  26.0 3.2 convolution_add_fusion.2
  30.4 7.3 %all-to-all-start = ((f32[2,128,512]{2,0,1:T(2,128)}), f32[2,128,512]{2,0,1:T(2,128)S(1)}, u32[]{:S(2)}, u32[]{:S(2)}) async-start(f32[2,128,512]{2,0,1:T(2,128)} %copy.57), calls=%async_computation | async-start | bytes 1048576 | tf_op jit(solution)/shard_map/all_to_all | solution.py:114
  37.7 9.6 %fusion.78 = (f32[512,1024]{1,0:T(8,128)S(1)}, f32[512,1024]{1,0:T(8,128)}) fusion(s32[512]{0:T(512)S(1)} %iota_add_fusion.6), kind=kLoop, calls=%fused_computation.130 | loop fusion | flops 7340032 | bytes 4196352 | tf_op jit(solution)/shard_map/cos | solution.py:32
  47.3 4.8 all-to-all-done
  53.6 47.6 %while.67 = (s32[]{:T(128)}, f32[32,1024]{1,0:T(8,128)S(1)}, f32[32,4096]{1,0:T(8,128)}, s32[]{:T(128)}, s32[]{:T(128)}, /*index=5*/s32[]{:T(128)}, s32[]{:T(128)}) while((s32[]{:T(128)}, f32[32,1024]{1,0:T(8,128)S(1)}, f32[32,4096]{1,0:T(8,128)}, s32[]{:T(128)}, s32[]{:T(128)}, /*index=5*/s32[]{:T(128)}, s32[]{:T(128)}) %tuple.197), condition=%wide.region_3.4_spmd.clone, body=%wide.region_2.3_spmd.clone.sunk | while | flops 412681728 | bytes 8794261 | solution.py:62
  53.9 8.3 %fusion.117 = (f32[1024,512]{1,0:T(8,128)S(1)}, f32[1024,512]{1,0:T(8,128)S(1)}) fusion(s32[512]{0:T(512)S(1)} %iota_add_fusion.17, s32[1024]{0:T(1024)S(1)} %iota_add_fusion.18), kind=kLoop, calls=%fused_computation.79.clone.1 | loop fusion | flops 7864320 | bytes 4200448 | tf_op jit(solution)/shard_map/while/body/eval_jaxpr/cos | solution.py:27
  62.2 3.5 fusion.118
  65.7 8.3 %fusion.117 = (f32[1024,512]{1,0:T(8,128)S(1)}, f32[1024,512]{1,0:T(8,128)S(1)}) fusion(s32[512]{0:T(512)S(1)} %iota_add_fusion.17, s32[1024]{0:T(1024)S(1)} %iota_add_fusion.18), kind=kLoop, calls=%fused_computation.79.clone.1 | loop fusion | flops 7864320 | bytes 4200448 | tf_op jit(solution)/shard_map/while/body/eval_jaxpr/cos | solution.py:27
  74.0 3.5 fusion.118
  77.6 8.3 %fusion.117 = (f32[1024,512]{1,0:T(8,128)S(1)}, f32[1024,512]{1,0:T(8,128)S(1)}) fusion(s32[512]{0:T(512)S(1)} %iota_add_fusion.17, s32[1024]{0:T(1024)S(1)} %iota_add_fusion.18), kind=kLoop, calls=%fused_computation.79.clone.1 | loop fusion | flops 7864320 | bytes 4200448 | tf_op jit(solution)/shard_map/while/body/eval_jaxpr/cos | solution.py:27
  85.9 3.5 fusion.118
  89.4 8.3 %fusion.117 = (f32[1024,512]{1,0:T(8,128)S(1)}, f32[1024,512]{1,0:T(8,128)S(1)}) fusion(s32[512]{0:T(512)S(1)} %iota_add_fusion.17, s32[1024]{0:T(1024)S(1)} %iota_add_fusion.18), kind=kLoop, calls=%fused_computation.79.clone.1 | loop fusion | flops 7864320 | bytes 4200448 | tf_op jit(solution)/shard_map/while/body/eval_jaxpr/cos | solution.py:27
  97.7 3.5 fusion.118
  101.3 6.2 %all_gather.6 = f32[2,64,512]{2,1,0:T(8,128)S(1)} all-gather(f32[2,16,512]{2,1,0:T(8,128)S(1)} %pad_maximum_fusion.7), channel_id=1, replica_groups=mesh['space'=8,'kern'=4] {'kern'}, dimensions={1}, use_global_device_ids=true | all-gather | bytes 327680 | tf_op jit(solution)/shard_map/all_gather | solution.py:115
  107.7 6.9 %fusion.61 = f32[2,64,4,2048]{3,1,2,0:T(8,128)S(1)} fusion(f32[512,1024]{1,0:T(8,128)S(1)} %copy-done.1, f32[512,1024]{1,0:T(8,128)S(1)} %get-tuple-element.572, f32[1,64,4,512]{3,1,2,0:T(8,128)S(1)} %get-tuple-element.563, f32[1,64,4,512]{3,1,2,0:T(8,128)S(1)} %get-tuple-element.562), kind=kOutput, calls=%fused_computation.97 | convolution fusion | flops 6443761664 | bytes 9437184 | tf_op jit(solution)/shard_map/dot_general | solution.py:123
  116.4 4.8 copy.60
  121.2 7.8 %reshape.172 = f32[8,1,65536]{2,1,0:T(1,128)} reshape(f32[1024,2,4,64]{3,2,1,0:T(4,128)} %bitcast.117) | data formatting | bytes 4194304
  129.0 53.8 %all_to_all.66 = f32[8,1,65536]{2,1,0:T(1,128)} all-to-all(f32[8,1,65536]{2,1,0:T(1,128)} %reshape.172), channel_id=1, replica_groups=mesh['space'=8,'kern'=4] {'space'}, dimensions={0} | all-to-all | bytes 4194304 | tf_op jit(solution)/shard_map/all_to_all | solution.py:132
  183.3 8.5 %reduce = f32[8,65536]{1,0:T(8,128)} reduce(f32[8,1,65536]{2,1,0:T(1,128)} %all_to_all.66, f32[]{:T(128)} %broadcast.377), dimensions={1}, to_apply=%all_to_all.51.reduce_sub_computation | reduce | bytes 4194308 | tf_op jit(solution)/shard_map/all_to_all | solution.py:132
  191.8 6.5 %reshape.173 = f32[1024,2,4,64]{3,2,1,0:T(4,128)} reshape(f32[8,65536]{1,0:T(8,128)} %reduce) | data formatting | bytes 4194304
  198.3 4.8 copy.61
  209.2 15.8 %fusion.59 = f32[2,4,128,2048]{3,2,1,0:T(8,128)S(1)} fusion(f32[2,4,128,512]{3,2,1,0:T(8,128)} %bitcast.122, f32[512,1024]{1,0:T(8,128)} %get-tuple-element.573, f32[512,1024]{1,0:T(8,128)S(1)} %get-tuple-element.572), kind=kOutput, calls=%fused_computation.95 | convolution fusion | flops 12885950464 | bytes 14680064 | tf_op jit(solution)/shard_map/dot_general | solution.py:134
  229.8 12.4 %collective-permute-done.1 = f32[128,1024]{1,0:T(8,128)S(1)} collective-permute-done((f32[128,1024]{1,0:T(8,128)S(1)}, f32[128,1024]{1,0:T(8,128)S(1)}, u32[]{:S(2)}, u32[]{:S(2)}) %collective-permute-start.1) | collective-permute-done | bytes 524320 | tf_op jit(solution)/shard_map/ppermute | solution.py:146
  245.1 3.9 maximum_bitcast_fusion
  249.0 15.5 %fusion.54 = f32[512,2,4,128]{3,0,2,1:T(8,128)S(1)} fusion(f32[1,4,128,2048]{3,2,1,0:T(8,128)} %get-tuple-element.561, f32[1,4,128,2048]{3,2,1,0:T(8,128)} %get-tuple-element.560, f32[512,1024]{1,0:T(8,128)S(1)} %copy-done.2, f32[512,1024]{1,0:T(8,128)S(1)} %get-tuple-element.572), kind=kOutput, calls=%fused_computation.86 | convolution fusion | flops 12888047616 | bytes 14680064 | tf_op jit(solution)/shard_map/dot_general | solution.py:161
  265.8 51.6 %all_to_all.67 = f32[512,2,4,128]{3,2,1,0:T(4,128)S(1)} all-to-all(f32[512,2,4,128]{3,2,1,0:T(4,128)S(1)} %copy.63), channel_id=1, replica_groups=mesh['space'=8,'kern'=4] {'space'}, dimensions={0} | all-to-all | bytes 4194304 | tf_op jit(solution)/shard_map/all_to_all | solution.py:163
  325.8 4.7 copy.65
  330.5 5.3 reshape.168
  335.8 8.9 %fusion.71 = f32[512,512]{1,0:T(8,128)S(1)} fusion(f32[512,2048]{1,0:T(8,128)} %reshape.168, f32[512,1024]{1,0:T(8,128)} %get-tuple-element.573, f32[512,1024]{1,0:T(8,128)S(1)} %get-tuple-element.572), kind=kOutput, calls=%fused_computation.117 | convolution fusion | flops 6443499520 | bytes 9437184 | tf_op jit(solution)/shard_map/dot_general | solution.py:173
  347.0 17.9 %reduce-scatter.3.cloned.1.call-done = f32[16,512]{1,0:T(8,128)} async-done(((f32[64,512]{1,0:T(8,128)}), f32[16,512]{1,0:T(8,128)}) %reduce-scatter.3.cloned.1.call-update) | async-done | bytes 32784 | tf_op jit(solution)/shard_map/reduce_scatter | solution.py:179
  365.7 22.0 %reduce-scatter.5.cloned.1.call-done = f32[16,512]{1,0:T(8,128)} async-done(((f32[64,512]{1,0:T(8,128)}), f32[16,512]{1,0:T(8,128)}) %reduce-scatter.5.cloned.1.call-update) | async-done | bytes 32784 | tf_op jit(solution)/shard_map/reduce_scatter | solution.py:180
  388.5 49.1 %while.64 = (s32[]{:T(128)}, f32[32,4096]{1,0:T(8,128)S(1)}, f32[32,1024]{1,0:T(8,128)S(1)}, s32[]{:T(128)}, s32[]{:T(128)}, /*index=5*/s32[]{:T(128)}, s32[]{:T(128)}) while((s32[]{:T(128)}, f32[32,4096]{1,0:T(8,128)S(1)}, f32[32,1024]{1,0:T(8,128)S(1)}, s32[]{:T(128)}, s32[]{:T(128)}, /*index=5*/s32[]{:T(128)}, ...), condition=%wide.region_10.11_spmd.clone, body=%wide.region_9.10_spmd.clone.sunk | while | flops 412616192 | bytes 8663171 | solution.py:83
  388.8 8.3 %fusion.108 = (f32[1024,512]{1,0:T(8,128)S(1)}, f32[1024,512]{1,0:T(8,128)S(1)}) fusion(s32[512]{0:T(512)S(1)} %iota_add_fusion.13, s32[1024]{0:T(1024)S(1)} %iota_add_fusion.14), kind=kLoop, calls=%fused_computation.20.clone.1 | loop fusion | flops 7864320 | bytes 4200448 | tf_op jit(solution)/shard_map/while/body/eval_jaxpr/cos | solution.py:27
  397.1 3.9 fusion.109
  401.0 8.3 %fusion.108 = (f32[1024,512]{1,0:T(8,128)S(1)}, f32[1024,512]{1,0:T(8,128)S(1)}) fusion(s32[512]{0:T(512)S(1)} %iota_add_fusion.13, s32[1024]{0:T(1024)S(1)} %iota_add_fusion.14), kind=kLoop, calls=%fused_computation.20.clone.1 | loop fusion | flops 7864320 | bytes 4200448 | tf_op jit(solution)/shard_map/while/body/eval_jaxpr/cos | solution.py:27
  409.3 3.9 fusion.109
  413.2 8.3 %fusion.108 = (f32[1024,512]{1,0:T(8,128)S(1)}, f32[1024,512]{1,0:T(8,128)S(1)}) fusion(s32[512]{0:T(512)S(1)} %iota_add_fusion.13, s32[1024]{0:T(1024)S(1)} %iota_add_fusion.14), kind=kLoop, calls=%fused_computation.20.clone.1 | loop fusion | flops 7864320 | bytes 4200448 | tf_op jit(solution)/shard_map/while/body/eval_jaxpr/cos | solution.py:27
  421.5 3.9 fusion.109
  425.5 8.3 %fusion.108 = (f32[1024,512]{1,0:T(8,128)S(1)}, f32[1024,512]{1,0:T(8,128)S(1)}) fusion(s32[512]{0:T(512)S(1)} %iota_add_fusion.13, s32[1024]{0:T(1024)S(1)} %iota_add_fusion.14), kind=kLoop, calls=%fused_computation.20.clone.1 | loop fusion | flops 7864320 | bytes 4200448 | tf_op jit(solution)/shard_map/while/body/eval_jaxpr/cos | solution.py:27
  433.8 3.9 fusion.109
  437.7 4.3 copy.70
  442.0 7.4 %reshape.174 = f32[8,1,16384]{2,1,0:T(1,128)S(1)} reshape(f32[4096,2,16]{2,1,0:T(2,128)} %bitcast.119) | data formatting | bytes 1048576
  449.5 19.3 %all_to_all.68 = f32[8,1,16384]{2,1,0:T(1,128)S(1)} all-to-all(f32[8,1,16384]{2,1,0:T(1,128)S(1)} %reshape.174), channel_id=1, replica_groups=mesh['space'=8,'kern'=4] {'space'}, dimensions={0} | all-to-all | bytes 1048576 | tf_op jit(solution)/shard_map/all_to_all | solution.py:183
  470.6 7.6 %reshape.175 = f32[4096,2,16]{2,1,0:T(2,128)} reshape(f32[8,16384]{1,0:T(8,128)S(1)} %reduce.1) | data formatting | bytes 1048576
  478.3 6.3 %copy.76 = f32[2,16,8,512]{3,1,2,0:T(8,128)} copy(f32[2,16,8,512]{1,0,3,2:T(2,128)} %bitcast.120) | data formatting | bytes 1048576 | tf_op jit(solution)/shard_map/all_to_all | solution.py:183
  484.6 20.8 %all-gather.2.cloned.1.call-done = f32[2,512,512]{2,1,0:T(8,128)} async-done(((f32[2,128,512]{2,1,0:T(8,128)}), f32[2,512,512]{2,1,0:T(8,128)}) %all-gather.2.cloned.1.call-update) | async-done | bytes 2097168 | tf_op jit(solution)/shard_map/all_gather | solution.py:190
  505.4 4.4 broadcast_in_dim.45.clone
  509.9 100.1 %while.65 = (s32[]{:T(128)}, f32[512,4096]{1,0:T(8,128)}, f32[1024,512]{1,0:T(8,128)}, s32[4,8]{1,0:T(4,128)S(1)}, s32[]{:T(128)}, /*index=5*/s32[]{:T(128)}, s32[]{:T(128)}, s32[]{:T(128)}) while((s32[]{:T(128)}, f32[512,4096]{1,0:T(8,128)}, f32[1024,512]{1,0:T(8,128)}, s32[4,8]{1,0:T(4,128)S(1)}, s32[]{:T(128)}, ...), condition=%wide.region_12.13_spmd.clone, body=%wide.region_11.12_spmd.clone.sunk | while | flops 6451890176 | bytes 39862572 | solution.py:97
  510.3 3.2 constant_dynamic-slice_fusion.2
  515.4 8.3 %fusion.112 = (f32[1024,512]{1,0:T(8,128)S(1)}, f32[1024,512]{1,0:T(8,128)S(1)}) fusion(s32[512]{0:T(512)S(1)} %sub.133, s32[1024]{0:T(1024)S(1)} %iota_add_fusion.15), kind=kLoop, calls=%fused_computation.39.clone.1 | loop fusion | flops 7864320 | bytes 4200448 | tf_op jit(solution)/shard_map/while/body/eval_jaxpr/cos | solution.py:22
  523.7 8.0 %bitcast_add_fusion.2 = f32[512,1024]{0,1:T(8,128)} fusion(f32[512,1024]{0,1:T(8,128)S(1)} %copy.92, f32[1024,512]{1,0:T(8,128)S(1)} %copy-done, f32[1024,512]{1,0:T(8,128)S(1)} %get-tuple-element.665, f32[1024,512]{1,0:T(8,128)S(1)} %get-tuple-element.666), kind=kOutput, calls=%fused_computation.37.clone.1 | convolution fusion | flops 6444023808 | bytes 10485760 | tf_op jit(solution)/shard_map/while/body/eval_jaxpr/dot_general | solution.py:93
  535.2 3.2 constant_dynamic-slice_fusion.2
  540.3 8.3 %fusion.112 = (f32[1024,512]{1,0:T(8,128)S(1)}, f32[1024,512]{1,0:T(8,128)S(1)}) fusion(s32[512]{0:T(512)S(1)} %sub.133, s32[1024]{0:T(1024)S(1)} %iota_add_fusion.15), kind=kLoop, calls=%fused_computation.39.clone.1 | loop fusion | flops 7864320 | bytes 4200448 | tf_op jit(solution)/shard_map/while/body/eval_jaxpr/cos | solution.py:22
  548.6 8.0 %bitcast_add_fusion.2 = f32[512,1024]{0,1:T(8,128)} fusion(f32[512,1024]{0,1:T(8,128)S(1)} %copy.92, f32[1024,512]{1,0:T(8,128)S(1)} %copy-done, f32[1024,512]{1,0:T(8,128)S(1)} %get-tuple-element.665, f32[1024,512]{1,0:T(8,128)S(1)} %get-tuple-element.666), kind=kOutput, calls=%fused_computation.37.clone.1 | convolution fusion | flops 6444023808 | bytes 10485760 | tf_op jit(solution)/shard_map/while/body/eval_jaxpr/dot_general | solution.py:93
  560.2 3.2 constant_dynamic-slice_fusion.2
  565.3 8.3 %fusion.112 = (f32[1024,512]{1,0:T(8,128)S(1)}, f32[1024,512]{1,0:T(8,128)S(1)}) fusion(s32[512]{0:T(512)S(1)} %sub.133, s32[1024]{0:T(1024)S(1)} %iota_add_fusion.15), kind=kLoop, calls=%fused_computation.39.clone.1 | loop fusion | flops 7864320 | bytes 4200448 | tf_op jit(solution)/shard_map/while/body/eval_jaxpr/cos | solution.py:22
  573.6 8.0 %bitcast_add_fusion.2 = f32[512,1024]{0,1:T(8,128)} fusion(f32[512,1024]{0,1:T(8,128)S(1)} %copy.92, f32[1024,512]{1,0:T(8,128)S(1)} %copy-done, f32[1024,512]{1,0:T(8,128)S(1)} %get-tuple-element.665, f32[1024,512]{1,0:T(8,128)S(1)} %get-tuple-element.666), kind=kOutput, calls=%fused_computation.37.clone.1 | convolution fusion | flops 6444023808 | bytes 10485760 | tf_op jit(solution)/shard_map/while/body/eval_jaxpr/dot_general | solution.py:93
  585.2 3.2 constant_dynamic-slice_fusion.2
  590.3 8.3 %fusion.112 = (f32[1024,512]{1,0:T(8,128)S(1)}, f32[1024,512]{1,0:T(8,128)S(1)}) fusion(s32[512]{0:T(512)S(1)} %sub.133, s32[1024]{0:T(1024)S(1)} %iota_add_fusion.15), kind=kLoop, calls=%fused_computation.39.clone.1 | loop fusion | flops 7864320 | bytes 4200448 | tf_op jit(solution)/shard_map/while/body/eval_jaxpr/cos | solution.py:22
  598.6 8.0 %bitcast_add_fusion.2 = f32[512,1024]{0,1:T(8,128)} fusion(f32[512,1024]{0,1:T(8,128)S(1)} %copy.92, f32[1024,512]{1,0:T(8,128)S(1)} %copy-done, f32[1024,512]{1,0:T(8,128)S(1)} %get-tuple-element.665, f32[1024,512]{1,0:T(8,128)S(1)} %get-tuple-element.666), kind=kOutput, calls=%fused_computation.37.clone.1 | convolution fusion | flops 6444023808 | bytes 10485760 | tf_op jit(solution)/shard_map/while/body/eval_jaxpr/dot_general | solution.py:93
  (123 shorter events, 65.6 us)
Async XLA Ops:
  30.4 21.7 %all-to-all-start = ((f32[2,128,512]{2,0,1:T(2,128)}), f32[2,128,512]{2,0,1:T(2,128)S(1)}, u32[]{:S(2)}, u32[]{:S(2)}) async-start(f32[2,128,512]{2,0,1:T(2,128)} %copy.57), calls=%async_computation | async-start | bytes 1048576 | tf_op jit(solution)/shard_map/all_to_all | solution.py:114
  37.6 327.3 %reduce-scatter.3.cloned.1.call-start = ((), (), s32[]{:S(2)}) async-start(), calls=%async_computation.6 | async-start | bytes 163840 | tf_op jit(solution)/shard_map/reduce_scatter | solution.py:179
  53.6 53.8 %copy-start.4 = (f32[2,4,64,512]{3,2,1,0:T(8,128)S(1)}, f32[2,4,64,512]{3,2,1,0:T(8,128)}, u32[]{:S(2)}) copy-start(f32[2,4,64,512]{3,2,1,0:T(8,128)} %param.12) | copy-start | bytes 3145732
  101.2 6.5 %copy-start.1 = (f32[512,1024]{1,0:T(8,128)S(1)}, f32[512,1024]{1,0:T(8,128)}, u32[]{:S(2)}) copy-start(f32[512,1024]{1,0:T(8,128)} %get-tuple-element.573) | copy-start | bytes 6291460
  226.1 16.2 %copy-start.5 = (s32[128,1024]{1,0:T(8,128)S(1)}, s32[128,1024]{1,0:T(8,128)}, u32[]{:S(2)}) copy-start(s32[128,1024]{1,0:T(8,128)} %param.13) | copy-start | bytes 1572868
  226.2 2.0 collective-permute-start
  228.2 14.0 %collective-permute-start.1 = (f32[128,1024]{1,0:T(8,128)S(1)}, f32[128,1024]{1,0:T(8,128)S(1)}, u32[]{:S(2)}, u32[]{:S(2)}) collective-permute-start(f32[128,1024]{1,0:T(8,128)S(1)} %fusion.87), channel_id=1, source_target_pairs={{0,2},{1,3},{2,0},{3,1},{4,6},{5,7},{6,4},{7,5},{8,10},{9,11},{10,... | collective-permute-start | bytes 1572872 | tf_op jit(solution)/shard_map/ppermute | solution.py:146
  245.1 3.9 copy-start.2
  322.7 1.9 copy-start.3
  346.2 41.4 %reduce-scatter.5.cloned.1.call-start = ((), (), s32[]{:S(2)}) async-start(), calls=%async_computation.7 | async-start | bytes 163840 | tf_op jit(solution)/shard_map/reduce_scatter | solution.py:180
  347.0 158.5 %all-gather.2.cloned.1.call-start = ((), (), s32[]{:S(2)}) async-start(), calls=%async_computation.8 | async-start | bytes 2621440 | tf_op jit(solution)/shard_map/all_gather | solution.py:190
  515.4 8.3 %copy-start = (f32[1024,512]{1,0:T(8,128)S(1)}, f32[1024,512]{1,0:T(8,128)}, u32[]{:S(2)}) copy-start(f32[1024,512]{1,0:T(8,128)} %get-tuple-element.762) | copy-start | bytes 6291460 | tf_op jit(solution)/shard_map/while
  540.3 8.3 %copy-start = (f32[1024,512]{1,0:T(8,128)S(1)}, f32[1024,512]{1,0:T(8,128)}, u32[]{:S(2)}) copy-start(f32[1024,512]{1,0:T(8,128)} %get-tuple-element.762) | copy-start | bytes 6291460 | tf_op jit(solution)/shard_map/while
  565.3 8.3 %copy-start = (f32[1024,512]{1,0:T(8,128)S(1)}, f32[1024,512]{1,0:T(8,128)}, u32[]{:S(2)}) copy-start(f32[1024,512]{1,0:T(8,128)} %get-tuple-element.762) | copy-start | bytes 6291460 | tf_op jit(solution)/shard_map/while
  590.2 8.3 %copy-start = (f32[1024,512]{1,0:T(8,128)S(1)}, f32[1024,512]{1,0:T(8,128)}, u32[]{:S(2)}) copy-start(f32[1024,512]{1,0:T(8,128)} %get-tuple-element.762) | copy-start | bytes 6291460 | tf_op jit(solution)/shard_map/while
Sparse Core Ops, SparseCore 0:
  346.3 18.5 reduce-scatter.2
  368.0 19.5 reduce-scatter.4
  484.7 20.7 all-gather.1
